TPU v7x, 512 devices: a whole 4x4x16 slice. The times are simulated.
512 devices in a mesh: row: 32 (over z, core), col: 16 (over x, y).
Axes of the slice: x: 4, y: 4, z: 16, core: 2. Of those that a mesh axis runs over, the one named last changes fastest.
Arguments:
- matrix: float32 [8192, 8192], P('row', 'col'), may hold values from -6 to 6
- pivots: int32 [3, 256], replicated, may hold values from 0 to 8191, as said below
- inverses: float32 [3, 256, 256], replicated, may hold values from -0.0234375 to 0.0234375
Outputs:
- factored: float32 [8192, 8192], P('row', 'col')
Inputs may be any that keep to these rules, and one draw needn't show every extreme that they name: For panel k and position i, pivots[k, i] is either k * 256 + i or a row of index (k + 1) * 256 or more; position 0 of every panel is k * 256; no row is named twice within one panel; every panel names row 8191.
All inputs are finite; a program needn't handle non-finite values.
Results may differ from a plain program's by a relative error of at most 0.00017.
Values sent between devices are 32-bit elements; how exact they have to be, the bound alone decides.
A program may use at most 64 MiB of HBM per device.

v0:
```python
import jax
import jax.numpy as jnp
from jax import lax
from jax.sharding import PartitionSpec as P


def broadcast(array, axis, root):
    mine = lax.axis_index(axis) == root
    return lax.psum(jnp.where(mine, array, jnp.zeros_like(array)), axis)


def on_device(matrix, pivots, inverses):
    rows_here, cols_here = matrix.shape
    block = inverses.shape[1]
    nrow = lax.axis_size("row")
    ncol = lax.axis_size("col")
    rank_row = lax.axis_index("row")
    rank_col = lax.axis_index("col")
    local_rows = jnp.arange(rows_here, dtype=jnp.int32)
    global_rows = (local_rows // block * nrow + rank_row) * block + local_rows % block
    col_index = jnp.arange(cols_here, dtype=jnp.int32)
    global_cblock = col_index // block * ncol + rank_col
    offsets = jnp.arange(block, dtype=jnp.int32)
    current = matrix
    for panel in range(pivots.shape[0]):
        top = panel * block
        chosen = pivots[panel]
        stay = chosen == top + offsets
        owner = chosen // block % nrow
        local_pick = chosen // block // nrow * block + chosen % block
        local_pick = jnp.clip(local_pick, 0, rows_here - 1)
        picked = jnp.where((owner == rank_row)[:, None], current[local_pick], 0.0)
        diag_owner = panel % nrow
        diag_local = panel // nrow * block
        diag_block = current
        upper = lax.psum(picked, "row")
        displaced = broadcast(diag_block, "row", diag_owner)
        matches = (global_rows[:, None] == chosen[None, :]) & jnp.logical_not(stay)[None, :]
        has_match = jnp.any(matches, axis=1)
        source = jnp.sum(jnp.where(matches, offsets[None, :], 0), axis=1)
        in_diag = (global_rows >= top) & (global_rows < top + block)
        diag_pos = jnp.clip(global_rows - top, 0, block - 1)
        swapped = jnp.where(
            has_match[:, None],
            displaced[source],
            jnp.where(in_diag[:, None], upper[diag_pos], current),
        )
        col_owner = panel % ncol
        col_local = panel // ncol * block
        strip = swapped[:, col_local : col_local + block]
        below = (global_rows >= top + block)[:, None]
        made = jnp.where(
            below,
            jnp.dot(
                strip,
                inverses[panel],
                precision=lax.Precision.HIGHEST,
                preferred_element_type=jnp.float32,
            ),
            0.0,
        )
        factor = broadcast(made, "col", col_owner)
        replaced = jnp.where(below & (rank_col == col_owner), factor, strip)
        swapped = swapped.at[:, col_local : col_local + block].set(replaced)
        update = jnp.dot(
            factor, upper, precision=lax.Precision.HIGHEST, preferred_element_type=jnp.float32
        )
        current = swapped - jnp.where((global_cblock > panel)[None, :], update, 0.0)
    return current


def solution(mesh):
    placed = (P("row", "col"), P(), P())
    return jax.shard_map(
        on_device, mesh=mesh, in_specs=placed, out_specs=P("row", "col"), check_vma=False
    )
```

profile of v0, /device:TPU:1, one launch (start us, length us, event | category | flops | bytes accessed | tf_op | source)
XLA Modules:
  0.0 1025.9 jit_solution(13716612972238767918)
XLA Ops:
  6.5 0.8 fusion.45
  7.4 0.3 select_reduce_fusion
  7.7 0.1 compare_select_fusion.1
  7.8 0.8 broadcast_select_fusion.5
  8.7 0.4 copy-done
  9.1 1.0 gather_fusion.1
  10.0 0.9 broadcast_select_fusion.4
  10.9 0.0 all-reduce.20.cloned.1.call-update
  11.0 0.0 all-reduce.10.cloned.1.call-start
  11.1 0.3 fusion.17
  11.4 215.7 %all-reduce.20.cloned.1.call-done = (f32[256,512]{1,0:T(8,128)}, f32[256,512]{1,0:T(8,128)}) async-done(((f32[256,512]{1,0:T(8,128)}, f32[256,512]{1,0:T(8,128)}), (f32[256,512]{1,0:T(8,128)}, f32[256,512]{1,0:T(8,128)})) %all-reduce.20.cloned.1.call-update) | async-done | bytes 1048592 | tf_op jit(solution)/shard_map/psum | solution.py:9
  227.1 2.3 gather_fusion
  229.4 1.0 gather_fusion.2
  230.4 0.1 select_select_fusion.2
  230.5 1.0 copy-done.7
  231.5 1.1 fusion.5
  232.6 0.0 all-reduce.10.cloned.1.call-update
  232.6 0.0 all-reduce.18.cloned.1.call-start
  232.7 0.7 compare_reduce_fusion
  233.4 112.8 %all-reduce.10.cloned.1.call-done = f32[256,256]{1,0:T(8,128)} async-done(((f32[256,256]{1,0:T(8,128)}), f32[256,256]{1,0:T(8,128)}) %all-reduce.10.cloned.1.call-update) | async-done | bytes 262160 | tf_op jit(solution)/shard_map/psum | solution.py:9
  346.1 1.7 fusion.6
  347.9 1.5 broadcast_select_fusion.3
  349.3 1.0 gather_fusion.4
  350.3 0.9 broadcast_select_fusion.2
  351.2 0.0 all-reduce.18.cloned.1.call-update
  351.2 0.0 all-reduce.12.cloned.1.call-start
  351.4 211.6 %all-reduce.18.cloned.1.call-done = (f32[256,512]{1,0:T(8,128)}, f32[256,512]{1,0:T(8,128)}) async-done(((f32[256,512]{1,0:T(8,128)}, f32[256,512]{1,0:T(8,128)}), (f32[256,512]{1,0:T(8,128)}, f32[256,512]{1,0:T(8,128)})) %all-reduce.18.cloned.1.call-update) | async-done | bytes 1048592 | tf_op jit(solution)/shard_map/psum | solution.py:9
  563.0 2.3 gather_fusion.3
  565.3 1.0 gather_fusion.5
  566.2 0.1 select_select_fusion.1
  566.4 1.1 fusion.4
  567.5 0.0 all-reduce.12.cloned.1.call-update
  567.5 0.0 all-reduce.16.cloned.1.call-start
  567.6 113.4 %all-reduce.12.cloned.1.call-done = f32[256,256]{1,0:T(8,128)} async-done(((f32[256,256]{1,0:T(8,128)}), f32[256,256]{1,0:T(8,128)}) %all-reduce.12.cloned.1.call-update) | async-done | bytes 262160 | tf_op jit(solution)/shard_map/psum | solution.py:9
  681.0 1.7 fusion.7
  682.8 1.5 broadcast_select_fusion.1
  684.2 1.0 gather_fusion.7
  685.2 0.9 broadcast_select_fusion
  686.1 0.0 all-reduce.16.cloned.1.call-update
  686.1 0.0 all-reduce.14.cloned.1.call-start
  686.3 211.6 %all-reduce.16.cloned.1.call-done = (f32[256,512]{1,0:T(8,128)}, f32[256,512]{1,0:T(8,128)}) async-done(((f32[256,512]{1,0:T(8,128)}, f32[256,512]{1,0:T(8,128)}), (f32[256,512]{1,0:T(8,128)}, f32[256,512]{1,0:T(8,128)})) %all-reduce.16.cloned.1.call-update) | async-done | bytes 1048592 | tf_op jit(solution)/shard_map/psum | solution.py:9
  897.8 2.3 gather_fusion.6
  900.2 1.0 gather_fusion.8
  901.1 0.1 select_select_fusion
  901.3 1.1 fusion.3
  902.4 113.5 %all-reduce.14.cloned.1.call-done = f32[256,256]{1,0:T(8,128)} async-done(((f32[256,256]{1,0:T(8,128)}), f32[256,256]{1,0:T(8,128)}) %all-reduce.14.cloned.1.call-update) | async-done | bytes 262160 | tf_op jit(solution)/shard_map/psum | solution.py:9
  1015.9 1.7 fusion.8
  1017.7 1.4 fusion
  (43 shorter events, 0.3 us)
Async XLA Ops:
  6.5 0.8 copy-start.8
  6.5 220.5 %all-reduce.20.cloned.1.call-start = ((), (), s32[]{:S(2)}) async-start(), calls=%async_computation.5 | async-start | bytes 2097152 | tf_op jit(solution)/shard_map/psum | solution.py:9
  7.8 1.2 copy-start
  11.0 335.2 %all-reduce.10.cloned.1.call-start = ((), (), s32[]{:S(2)}) async-start(), calls=%async_computation | async-start | bytes 524288 | tf_op jit(solution)/shard_map/psum | solution.py:9
  227.1 2.3 copy-start.1
  230.4 1.1 copy-start.7
  232.6 330.3 %all-reduce.18.cloned.1.call-start = ((), (), s32[]{:S(2)}) async-start(), calls=%async_computation.4 | async-start | bytes 2097152 | tf_op jit(solution)/shard_map/psum | solution.py:9
  346.1 1.7 copy-start.4
  351.2 329.8 %all-reduce.12.cloned.1.call-start = ((), (), s32[]{:S(2)}) async-start(), calls=%async_computation.1 | async-start | bytes 524288 | tf_op jit(solution)/shard_map/psum | solution.py:9
  563.0 2.3 copy-start.2
  567.5 330.3 %all-reduce.16.cloned.1.call-start = ((), (), s32[]{:S(2)}) async-start(), calls=%async_computation.3 | async-start | bytes 2097152 | tf_op jit(solution)/shard_map/psum | solution.py:9
  681.0 1.7 copy-start.5
  686.1 329.8 %all-reduce.14.cloned.1.call-start = ((), (), s32[]{:S(2)}) async-start(), calls=%async_computation.2 | async-start | bytes 524288 | tf_op jit(solution)/shard_map/psum | solution.py:9
  897.8 2.3 copy-start.3
  1015.9 1.7 copy-start.6
Sparse Core Ops, SparseCore 0:
  11.1 215.9 all-reduce.19
  232.7 113.3 all-reduce.9
  351.4 211.5 all-reduce.17
  567.6 113.3 all-reduce.11
  686.3 211.5 all-reduce.15
  902.5 113.3 all-reduce.13
where the time goes:
time: 1030 us
  waiting for transfers between devices  979 us (95%)
  local copies, waits for them, and re-layouts  15 us (1%)
  between operations  13.8 us (1%)
  other arithmetic  10.7 us (1%)
    psum x6, waiting for transfers between devices, broadcast(): return lax.psum(jnp.where(mine, array, jnp.zeros_like(array)), axis)  979 us
  transfers between devices with their start and end apart: 6, of which 6 were waited for; matrix products, arithmetic and copies ran while one was open for 0% of the time, Pallas kernels for 0%

commit v1 on v0

v1 whole, which is shorter than its diff:
```python
import functools

import jax
import jax.numpy as jnp
from jax import lax
from jax.experimental import pallas as pl
from jax.experimental.pallas import tpu as pltpu
from jax.sharding import PartitionSpec as P

MESH = pl.DeviceIdType.MESH
F32 = jnp.float32
BF16 = jnp.bfloat16
NX, NY = 4, 4


def dot(a, b):
    return jnp.dot(a, b, preferred_element_type=F32)


def split2(a):
    hi = a.astype(BF16)
    return hi, (a - hi.astype(F32)).astype(BF16)


def split3(a):
    hi = a.astype(BF16)
    rest = a - hi.astype(F32)
    mid = rest.astype(BF16)
    return hi, mid, (rest - mid.astype(F32)).astype(BF16)


def mm(a, b):
    ah, al = split2(a)
    bh, bl = split2(b)
    return dot(ah, bh) + (dot(ah, bl) + dot(al, bh))


def select_rows(onehot, b):
    hi, mid, lo = split3(b)
    return dot(onehot, hi) + dot(onehot, mid) + dot(onehot, lo)


def kernel(
    nz, nb,
    a_ref, piv_ref, inv_ref, o_ref,
    B, Pt, SG, DG, TG, XG, NBf, rp, rm, sp, sm, Y,
    ex_s, ex_r, ds_s, ds_r, rs_s, rs_r, dg_s, dg_r, sg_s, sg_r, tg_s, tg_r, fw_s, fw_r,
    t1_s, t1_r, t2_s, t2_r, x1_s, x1_r, x2_s, x2_r, x3_s, x3_r, out_s, out_r,
):
    row = lax.axis_index("row")
    q = lax.axis_index("col")
    z, c = row // 2, row % 2
    x, y = q // NY, q % NY
    ch = nb // nz
    up, down = 2 * ((z + 1) % nz) + c, 2 * ((z + nz - 1) % nz) + c
    sib = 2 * z + 1 - c
    source = jnp.logical_and(jnp.logical_and(x == 0, y < 3), c == 0)

    def dev(r, k):
        return {"row": r, "col": k}

    def remote(src, dst, ss, rs, r, k):
        return pltpu.make_async_remote_copy(
            src_ref=src, dst_ref=dst, send_sem=ss, recv_sem=rs,
            device_id=dev(r, k), device_id_type=MESH,
        )

    bar = pltpu.get_barrier_semaphore()

    def greet(r, k):
        pl.semaphore_signal(bar, inc=1, device_id=dev(r, k), device_id_type=MESH)

    greet(sib, q)
    greet(up, q)
    greet(down, q)
    for d in range(1, NY):
        greet(row, x * NY + (y + d) % NY)

    @pl.when(z != 0)
    def _():
        greet(c, q)

    @pl.when(z != 1)
    def _():
        greet(2 + c, q)

    @pl.when(jnp.logical_and(x != 0, y < 3))
    def _():
        greet(2 * z, y)

    expected = (
        3 + (NY - 1)
        + jnp.where(z <= 1, nz - 1, 0)
        + jnp.where(source, 2 * (NX - 1), 0)
    )
    pl.semaphore_wait(bar, expected)

    other = pl.multiple_of((1 - c) * nb, nb)
    mine = pl.multiple_of(c * nb, nb)
    swap = remote(a_ref.at[:, pl.ds(other, nb)], B.at[c], ex_s, ex_r, sib, q)
    swap.start()
    B[c] = a_ref[:, pl.ds(mine, nb)]

    lane = lax.broadcasted_iota(jnp.int32, (nb, nb), 1)
    subl = lax.broadcasted_iota(jnp.int32, (nb, nb), 0)
    prow = [piv_ref[k:k + 1, :].astype(F32) for k in range(3)]
    eye = lane == subl
    pcol = [
        jnp.max(jnp.where(eye, jnp.broadcast_to(p, (nb, nb)), -1.0), axis=1, keepdims=True)
        for p in prow
    ]
    lanef = lane.astype(F32)

    def back(v, k):
        n = v.shape[0]
        hit = jnp.where(
            jnp.broadcast_to(v, (n, nb)) == jnp.broadcast_to(prow[k], (n, nb)),
            lanef[:1, :] + float(k * nb), -1.0,
        )
        best = jnp.max(hit, axis=1, keepdims=True)
        return jnp.where(best >= 0.0, best, v)

    slots = [pcol[0], back(pcol[1], 0), back(back(pcol[2], 1), 0)]
    base = (z * 2 * nb).astype(F32)
    own = [
        subl[:, :1].astype(F32) + base + float(h * nb) for h in range(2)
    ]
    came = [back(back(back(g, 2), 1), 0) for g in own]
    here = lax.broadcasted_iota(jnp.int32, (nb, 2 * nb), 1).astype(F32) + base

    swap.wait()

    def share(d):
        to = (z + d) % nz
        rows = pl.ds(pl.multiple_of(to * ch, ch), ch)
        return to, rows

    @pl.when(z == 0)
    def _():
        for d in range(1, nz):
            to, rows = share(d)
            remote(B.at[:, rows], DG.at[pl.ds(0, 2), rows], ds_s.at[d], ds_r.at[0], 2 * to + c, q).start()
        DG[0:2, 0:ch] = B[:, 0:ch]

    @pl.when(z == 1)
    def _():
        for d in range(1, nz):
            to, rows = share(d)
            remote(
                B.at[pl.ds(0, 1), rows], DG.at[pl.ds(2, 1), rows], ds_s.at[d], ds_r.at[1], 2 * to + c, q
            ).start()
        DG[2, ch:2 * ch] = B[0, ch:2 * ch]

    parts = split3(B[...].reshape(2 * nb, nb))
    for k in range(3):
        oh = (jnp.broadcast_to(slots[k], (nb, 2 * nb)) == here).astype(F32).astype(BF16)
        Pt[k] = dot(oh, parts[0]) + dot(oh, parts[1]) + dot(oh, parts[2])

    def chunk(i):
        return pl.ds(pl.multiple_of(lax.rem(i + 2 * nz, nz) * ch, ch), ch)

    half = nz // 2

    def rs_step(t):
        rows = chunk(z + half - t)
        sp[t] = Pt[:, rows] if t == 0 else Pt[:, rows] + rp[t - 1]
        cps = [remote(sp.at[t], rp.at[t], rs_s.at[0], rs_r.at[0, t], up, q)]
        if t < half - 1:
            rows = chunk(z - (half - 1) + t)
            sm[t] = Pt[:, rows] if t == 0 else Pt[:, rows] + rm[t - 1]
            cps.append(remote(sm.at[t], rm.at[t], rs_s.at[1], rs_r.at[1, t], down, q))
        for cp in cps:
            cp.start()
        return cps

    def ag_step(buf, t, ss, rs):
        rows = chunk(z - t)
        cps = [remote(buf.at[:, rows], buf.at[:, rows], ss.at[0], rs.at[0, t], up, q)]
        if t < half - 1:
            rows = chunk(z + t)
            cps.append(remote(buf.at[:, rows], buf.at[:, rows], ss.at[1], rs.at[1, t], down, q))
        for cp in cps:
            cp.start()
        return cps

    tmine = TG.at[pl.ds(3 * c, 3)]

    def fwd(slot, i):
        rows = chunk(i)
        cp = remote(tmine.at[:, rows], tmine.at[:, rows], fw_s.at[slot], fw_r.at[slot], sib, q)
        cp.start()
        return cp

    forwards = []
    lag_d = min(3, half - 1)
    lag_s = half
    lag_t = half + lag_d
    for tick in range(lag_t + half):
        cps = []
        if tick < half:
            cps += rs_step(tick)
        if tick == lag_d:
            @pl.when(z == 0)
            def _():
                for d in range(1, nz):
                    to, rows = share(d)
                    remote(
                        B.at[:, rows], DG.at[pl.ds(0, 2), rows], ds_s.at[d], ds_r.at[0], 2 * to + c, q
                    ).wait_send()

            @pl.when(z == 1)
            def _():
                for d in range(1, nz):
                    to, rows = share(d)
                    remote(
                        B.at[pl.ds(0, 1), rows], DG.at[pl.ds(2, 1), rows], ds_s.at[d], ds_r.at[1], 2 * to + c, q
                    ).wait_send()

            rows = chunk(z)

            @pl.when(z != 0)
            def _():
                remote(B.at[:, rows], DG.at[pl.ds(0, 2), rows], ds_s.at[0], ds_r.at[0], up, q).wait_recv()

            @pl.when(z != 1)
            def _():
                remote(
                    B.at[pl.ds(0, 1), rows], DG.at[pl.ds(2, 1), rows], ds_s.at[0], ds_r.at[1], up, q
                ).wait_recv()
        if lag_d <= tick < lag_d + half:
            cps += ag_step(DG, tick - lag_d, dg_s, dg_r)
        if tick == lag_s:
            rows = chunk(z)
            total = Pt[:, rows] + rp[half - 1] + rm[half - 2]
            SG[:, rows] = total

            @pl.when(source)
            def _():
                first = jnp.where(y == 0, 1, 0)
                second = jnp.where(y == 2, 1, 2)
                for d in range(1, NX):
                    remote(SG.at[first, rows], TG.at[y, rows], t1_s.at[0, d], t1_r, 2 * z, d * NY + y).start()
                for d in range(NX):
                    remote(
                        SG.at[second, rows], TG.at[3 + y, rows], t1_s.at[1, d], t1_r, 2 * z + 1, d * NY + y
                    ).start()
                TG[y, rows] = SG[first, rows]
        if lag_s <= tick < lag_s + half:
            cps += ag_step(SG, tick - lag_s, sg_s, sg_r)
        if tick == lag_s + 1:

            @pl.when(y < 3)
            def _():
                rows = chunk(z)
                piece = TG.at[3 * c + y, rows]

                @pl.when(jnp.logical_not(source))
                def _():
                    remote(piece, piece, t1_s.at[0, 0], t1_r, row, y).wait_recv()

                for d in range(1, NY):
                    remote(piece, piece, t2_s.at[d], t2_r.at[y], row, x * NY + (y + d) % NY).start()

        if tick == lag_t:
            rows = chunk(z)
            for j in range(3):
                @pl.when(y != j)
                def _(j=j):
                    piece = TG.at[3 * c + j, rows]
                    remote(piece, piece, t2_s.at[0], t2_r.at[j], row, q).wait_recv()
            forwards.append(fwd(0, z))
            dg = split3(DG[...].reshape(3 * nb, nb))
            there = lax.broadcasted_iota(jnp.int32, (nb, 3 * nb), 1).astype(F32)
            for h in range(2):
                oh = (jnp.broadcast_to(came[h], (nb, 3 * nb)) == there).astype(F32).astype(BF16)
                moved = dot(oh, dg[0]) + dot(oh, dg[1]) + dot(oh, dg[2])
                keep = jnp.broadcast_to(came[h], (nb, nb)) == jnp.broadcast_to(own[h], (nb, nb))
                NBf[h] = jnp.where(keep, B[h], moved)

            @pl.when(source)
            def _():
                for d in range(1, NX):
                    remote(NBf.at[0], XG.at[y, 0], x1_s.at[0, d], x1_r, 2 * z, d * NY + y).start()
                for d in range(NX):
                    remote(NBf.at[1], XG.at[y, 1], x1_s.at[1, d], x1_r, 2 * z + 1, d * NY + y).start()
                XG[y, 0] = NBf[0]
        if tick >= lag_t:
            cps += ag_step(tmine, tick - lag_t, tg_s, tg_r)
        if tick == lag_t + min(3, half - 2):
            @pl.when(y < 3)
            def _():
                piece = XG.at[y, c]

                @pl.when(jnp.logical_not(source))
                def _():
                    remote(piece, piece, x1_s.at[0, 0], x1_r, row, y).wait_recv()

                for d in range(1, NY):
                    remote(piece, piece, x2_s.at[d], x2_r.at[y], row, x * NY + (y + d) % NY).start()
        for cp in cps:
            cp.wait()
        if tick >= lag_t:
            t = tick - lag_t
            forwards.append(fwd(1 + t, z - 1 - t))
            if t < half - 1:
                forwards.append(fwd(1 + half + t, z + 1 + t))

    for j in range(3):
        @pl.when(y != j)
        def _(j=j):
            piece = XG.at[j, c]
            remote(piece, piece, x2_s.at[0], x2_r.at[j], row, q).wait_recv()
    strips = remote(XG.at[:, c], XG.at[:, c], x3_s, x3_r, sib, q)
    strips.start()
    strips.wait()
    for cp in forwards:
        cp.wait()

    i0, i1, i2 = inv_ref[0], inv_ref[1], inv_ref[2]
    t10, t01, t02, t20, t21, t12 = (TG[j] for j in range(6))
    l10, l20 = mm(t10, i0), mm(t20, i0)
    l21 = mm(t21 - mm(l20, t01), i1)
    u12 = t12 - mm(l10, t02)
    u0 = SG[0]
    u1 = SG[1] - mm(l10, u0)
    u2 = SG[2] - mm(l20, u0) - mm(l21, u1)
    panel_col = jnp.logical_and(c == 0, q < 3)
    for h in range(2):
        l0 = mm(XG[0, h], i0)
        l1 = mm(XG[1, h] - mm(l0, t01), i1)
        l2 = mm(XG[2, h] - mm(l0, t02) - mm(l1, u12), i2)
        Y[h] = NBf[h] - mm(l0, u0) - mm(l1, u1) - mm(l2, u2)
        for k, l in enumerate((l0, l1, l2)):
            @pl.when(jnp.logical_and(panel_col, q == k))
            def _(h=h, l=l):
                Y[h] = l
        for r, u in enumerate((u0, u1, u2)):
            if r % 2 != h:
                continue

            @pl.when(row // 2 * 2 + h == r)
            def _(h=h, u=u):
                Y[h] = u
        for r, k, l in ((1, 0, l10), (2, 0, l20), (2, 1, l21)):
            if r % 2 != h:
                continue

            @pl.when(jnp.logical_and(row // 2 * 2 + h == r, jnp.logical_and(panel_col, q == k)))
            def _(h=h, l=l):
                Y[h] = l

    back_copy = remote(Y.at[1 - c], o_ref.at[:, pl.ds(mine, nb)], out_s, out_r, sib, q)
    back_copy.start()
    o_ref[:, pl.ds(mine, nb)] = Y[c]
    back_copy.wait()

    @pl.when(source)
    def _():
        rows = chunk(z)
        for d in range(1, NX):
            remote(SG.at[0, rows], TG.at[y, rows], t1_s.at[0, d], t1_r, 2 * z, d * NY + y).wait_send()
            remote(NBf.at[0], XG.at[y, 0], x1_s.at[0, d], x1_r, 2 * z, d * NY + y).wait_send()
        for d in range(NX):
            remote(SG.at[0, rows], TG.at[3 + y, rows], t1_s.at[1, d], t1_r, 2 * z + 1, d * NY + y).wait_send()
            remote(NBf.at[1], XG.at[y, 1], x1_s.at[1, d], x1_r, 2 * z + 1, d * NY + y).wait_send()

    @pl.when(y < 3)
    def _():
        rows = chunk(z)
        for d in range(1, NY):
            to = x * NY + (y + d) % NY
            piece = TG.at[3 * c + y, rows]
            remote(piece, piece, t2_s.at[d], t2_r.at[y], row, to).wait_send()
            piece = XG.at[y, c]
            remote(piece, piece, x2_s.at[d], x2_r.at[y], row, to).wait_send()


def on_device(matrix, pivots, inverses):
    nb = inverses.shape[1]
    nz = lax.axis_size("row") // 2
    ch = nb // nz
    half = nz // 2
    DMA = pltpu.SemaphoreType.DMA

    def vm(*shape):
        return pltpu.VMEM(shape, F32)

    return pl.pallas_call(
        functools.partial(kernel, nz, nb),
        out_shape=jax.ShapeDtypeStruct(matrix.shape, matrix.dtype),
        in_specs=[pl.BlockSpec(memory_space=pltpu.VMEM)] * 3,
        out_specs=pl.BlockSpec(memory_space=pltpu.VMEM),
        scratch_shapes=[
            vm(2, nb, nb), vm(3, nb, nb), vm(3, nb, nb), vm(3, nb, nb), vm(6, nb, nb),
            vm(3, 2, nb, nb), vm(2, nb, nb),
            vm(half, 3, ch, nb), vm(half - 1, 3, ch, nb), vm(half, 3, ch, nb), vm(half - 1, 3, ch, nb),
            vm(2, nb, nb),
            DMA, DMA, DMA((nz,)), DMA((2,)),
            DMA((2,)), DMA((2, half)), DMA((2,)), DMA((2, half)),
            DMA((2,)), DMA((2, half)), DMA((2,)), DMA((2, half)),
            DMA((2 * half,)), DMA((2 * half,)),
            DMA((2, NX)), DMA, DMA((NY,)), DMA((3,)),
            DMA((2, NX)), DMA, DMA((NY,)), DMA((3,)),
            DMA, DMA, DMA, DMA,
        ],
        compiler_params=pltpu.CompilerParams(
            collective_id=0, has_side_effects=True, vmem_limit_bytes=48 * 2**20
        ),
        name="panels",
    )(matrix, pivots, inverses)


def solution(mesh):
    placed = (P("row", "col"), P(), P())
    return jax.shard_map(
        on_device, mesh=mesh, in_specs=placed, out_specs=P("row", "col"), check_vma=False
    )
```

time: 1030 us -> 117 us (0.11)
  waiting for transfers between devices: 979 us -> 0 us
  Pallas kernels: 0 us -> 113 us
  between operations: 13.8 us -> 0.01 us
  local copies, waits for them, and re-layouts: 15 us -> 3.66 us
  other arithmetic: 10.7 us -> 0 us
    psum x6 -> x0, waiting for transfers between devices: 979 us -> none  [broadcast(): return lax.psum(jnp.where(mine, array, jnp.zeros_like(array)), axis)]
    pallas_call x0 -> x1, Pallas kernels: none -> 113 us  [on_device(): pl.pallas_call(functools.partial(kernel, nz, nb), out_shape=jax.ShapeDtyp...]
    gather x9 -> x0, local copies, waits for them, and re-layouts: 12.7 us -> none  [the longest x3 6.92 us: on_device(): displaced[source]]
  transfers between devices with their start and end apart: 6 -> 0, of which waited for: 6 -> 0; matrix products, arithmetic and copies ran while one was open for 0% -> 0% of each run, Pallas kernels for 0% -> 0%
where the time goes in v1:
time: 117 us
  Pallas kernels  113 us (97%)
  local copies, waits for them, and re-layouts  3.66 us (3%)
    pallas_call x1, Pallas kernels, on_device(): pl.pallas_call(functools.partial(kernel, nz, nb), out_shape=jax.ShapeDtyp...  113 us
    unnamed x7, local copies, waits for them, and re-layouts  3.66 us

profile of v1, /device:TPU:1, one launch (start us, length us, event | category | flops | bytes accessed | tf_op | source)
XLA Modules:
  0.0 117.1 jit_solution(12640143625246545207)
XLA Ops:
  0.0 0.0 copy-start
  0.0 1.1 copy-done
  1.1 0.0 copy-start.1
  1.1 1.0 copy-done.1
  2.2 0.0 copy-start.2
  2.2 0.7 copy-done.2
  2.9 113.4 %panels.1 = f32[256,512]{1,0:T(8,128)S(1)} custom-call(f32[256,512]{1,0:T(8,128)S(1)} %copy-done.1, s32[3,256]{1,0:T(4,128)S(1)} %copy-done.2, f32[3,256,256]{2,1,0:T(8,128)S(1)} %copy-done), custom_call_target="tpu_custom_call" | custom-call | tf_op jit(solution)/shard_map/panels/pallas_call | solution.py:388
  116.3 0.8 copy.5
Async XLA Ops:
  0.0 1.1 copy-start
  1.1 1.0 copy-start.1
  2.2 0.7 copy-start.2

commit v2 on v1

v2 whole, which is shorter than its diff:
```python
import functools

import jax
import jax.numpy as jnp
from jax import lax
from jax.experimental import pallas as pl
from jax.experimental.pallas import tpu as pltpu
from jax.sharding import PartitionSpec as P

MESH = pl.DeviceIdType.MESH
F32 = jnp.float32
BF16 = jnp.bfloat16
NX, NY = 4, 4
RING = ((0, 1, 2, 3, 4, 5, 6, 7, 8), (0, -1, -2, -3, -4, -5, -6, -7))
RS_WAY, D_WAY, S_WAY, T_WAY = RING, RING, RING, RING
AT_D, AT_S, AT_T2, AT_T, AT_X2 = 4, 8, 9, 10, 15
PER, PX = 5, 2


def dot(a, b):
    return jnp.dot(a, b, preferred_element_type=F32)


def split2(a):
    hi = a.astype(BF16)
    return hi, (a - hi.astype(F32)).astype(BF16)


def split3(a):
    hi = a.astype(BF16)
    rest = a - hi.astype(F32)
    mid = rest.astype(BF16)
    return hi, mid, (rest - mid.astype(F32)).astype(BF16)


def mm(a, b):
    ah, al = split2(a)
    bh, bl = split2(b)
    return dot(ah, bh) + (dot(ah, bl) + dot(al, bh))


def select_rows(onehot, b):
    hi, mid, lo = split3(b)
    return dot(onehot, hi) + dot(onehot, mid) + dot(onehot, lo)


def kernel(
    nz, nb,
    a_ref, piv_hbm, inv_hbm, o_ref,
    piv_ref, inv_ref, sm_s,
    B, Pt, SG, DG, TG, XG, NBf, NX_, got, put,
    ld_s, ex_s, ex_r, ds_s, ds_r, rs_s, rs_r, dg_s, dg_r, sg_s, sg_r, tg_s, tg_r, ft_s, ft_r, fs_s, fs_r,
    t1_s, t1_r, t2_s, t2_r, x1_s, x1_r, x2_s, x2_r, nx_s, nx_r,
):
    row = lax.axis_index("row")
    q = lax.axis_index("col")
    z, c = row // 2, row % 2
    x, y = q // NY, q % NY
    ch = nb // nz
    up = 2 * ((z + 1) % nz) + c
    sib = 2 * z + 1 - c
    source = jnp.logical_and(jnp.logical_and(x == 0, y < 3), c == 0)

    def dev(r, k):
        return {"row": r, "col": k}

    def remote(src, dst, ss, rs, r, k):
        return pltpu.make_async_remote_copy(
            src_ref=src, dst_ref=dst, send_sem=ss, recv_sem=rs,
            device_id=dev(r, k), device_id_type=MESH,
        )

    other = pl.multiple_of((1 - c) * nb, nb)
    mine = pl.multiple_of(c * nb, nb)
    load = pltpu.make_async_copy(a_ref.at[:, pl.ds(mine, nb)], B.at[c], ld_s)
    load.start()
    load_piv = pltpu.make_async_copy(piv_hbm, piv_ref, sm_s.at[0])
    load_inv = pltpu.make_async_copy(inv_hbm, inv_ref, sm_s.at[1])
    load_piv.start()
    load_inv.start()

    bar = pltpu.get_barrier_semaphore()

    def greet(r, k):
        pl.semaphore_signal(bar, inc=1, device_id=dev(r, k), device_id_type=MESH)

    greet(sib, q)
    for d in (1, 2, nz - 1, nz - 2):
        greet(2 * ((z + d) % nz) + c, q)
    for d in range(1, NY):
        greet(row, x * NY + (y + d) % NY)

    @pl.when(z != 0)
    def _():
        greet(c, q)

    @pl.when(z != 1)
    def _():
        greet(2 + c, q)

    @pl.when(jnp.logical_and(x != 0, y < 3))
    def _():
        greet(2 * z, y)

    expected = (
        5 + (NY - 1)
        + jnp.where(z <= 1, nz - 1, 0)
        + jnp.where(source, 2 * (NX - 1), 0)
    )
    pl.semaphore_wait(bar, expected)
    swap = remote(a_ref.at[:, pl.ds(other, nb)], B.at[c], ex_s, ex_r, sib, q)
    swap.start()
    load_piv.wait()
    lane = lax.broadcasted_iota(jnp.int32, (nb, nb), 1)
    subl = lax.broadcasted_iota(jnp.int32, (nb, nb), 0)
    prow = [piv_ref[k:k + 1, :].astype(F32) for k in range(3)]
    eye = lane == subl
    pcol = [
        jnp.max(jnp.where(eye, jnp.broadcast_to(p, (nb, nb)), -1.0), axis=1, keepdims=True)
        for p in prow
    ]
    lanef = lane.astype(F32)

    def back(v, k):
        n = v.shape[0]
        hit = jnp.where(
            jnp.broadcast_to(v, (n, nb)) == jnp.broadcast_to(prow[k], (n, nb)),
            lanef[:1, :] + float(k * nb), -1.0,
        )
        best = jnp.max(hit, axis=1, keepdims=True)
        return jnp.where(best >= 0.0, best, v)

    slots = [pcol[0], back(pcol[1], 0), back(back(pcol[2], 1), 0)]
    base = (z * 2 * nb).astype(F32)
    own = [subl[:, :1].astype(F32) + base + float(h * nb) for h in range(2)]
    came = [back(back(back(g, 2), 1), 0) for g in own]
    here = lax.broadcasted_iota(jnp.int32, (nb, 2 * nb), 1).astype(F32) + base

    load.wait()
    swap.wait_recv()

    def ring(i):
        return lax.rem(i + 2 * nz, nz)

    def share(which, d):
        i = ring(z + d)
        rows = pl.ds(pl.multiple_of(i * ch, ch), ch)
        if which == 0:
            return remote(B.at[:, rows], DG.at[i, pl.ds(0, 2)], ds_s.at[d], ds_r.at[0], 2 * i + c, q)
        return remote(B.at[pl.ds(0, 1), rows], DG.at[i, pl.ds(2, 1)], ds_s.at[d], ds_r.at[1], 2 * i + c, q)

    far_first = sorted(range(1, nz), key=lambda d: -min(d, nz - d))

    @pl.when(z == 0)
    def _():
        DG[0, 0:2] = B[:, 0:ch]

    @pl.when(z == 1)
    def _():
        DG[1, 2] = B[0, ch:2 * ch]

    parts = split3(B[...].reshape(2 * nb, nb))
    for k in range(3):
        oh = (jnp.broadcast_to(slots[k], (nb, 2 * nb)) == here).astype(F32).astype(BF16)
        part = dot(oh, parts[0]) + dot(oh, parts[1]) + dot(oh, parts[2])
        Pt[:, k] = part.reshape(nz, ch, nb)

    sent = []
    def begin(cp):
        cp.start()
        sent.append(cp)
        return cp

    flight = {}

    def chip(d):
        return 2 * ring(z + d) + c

    def rs_step(t):
        for w, route in enumerate(RS_WAY):
            n = len(route) - 1
            at = sum(len(r) - 1 for r in RS_WAY[:w]) + t
            if 0 < t <= n:
                flight.pop(("rs", w)).wait_recv()
            if t < n:
                far = route[n - t]
                i = ring(z + far)
                put[at] = Pt[i] if t == 0 else Pt[i] + got[at - 1]
                flight["rs", w] = begin(
                    remote(put.at[at], got.at[at], rs_s.at[at], rs_r.at[at], chip(far - route[n - t - 1]), q)
                )

    def ag_step(name, way, buf, t, ss, rs, forward=None):
        if t == 0 and forward is not None:
            forward(0, z)
        for w, route in enumerate(way):
            n = len(route) - 1
            at = sum(len(r) - 1 for r in way[:w]) + t
            if 0 < t <= n:
                flight.pop((name, w)).wait_recv()
            if t < n:
                i = ring(z - route[t])
                flight[name, w] = begin(
                    remote(buf.at[i], buf.at[i], ss.at[at], rs.at[at], chip(route[t + 1] - route[t]), q)
                )
            if forward is not None and 0 < t <= n:
                forward(at, z - route[t])

    tmine = TG.at[c]
    smine = SG.at[c]
    crossing = []

    def to_sibling(buf, ss, rs):
        def forward(slot, i):
            i = ring(i)
            cp = begin(remote(buf.at[i], buf.at[i], ss.at[slot], rs.at[slot], sib, q))
            crossing.append(cp)
        return forward

    def part(p):
        return pl.ds(p * (nb // PX), nb // PX)

    def strips(p):
        for d in range(NX):
            for h in range(2):
                if d or h:
                    yield h, d, remote(
                        NBf.at[h, part(p)], XG.at[y, part(p)], x1_s.at[h, d, p], x1_r.at[p], 2 * z + h, d * NY + y
                    )

    def strips_y(d, p):
        piece = XG.at[y, part(p)]
        return remote(piece, piece, x2_s.at[d, p], x2_r.at[y, p], row, x * NY + (y + d) % NY)

    def rounds(way):
        return max(len(r) for r in way) - 1

    n_rs, n_d, n_s, n_t = rounds(RS_WAY), rounds(D_WAY), rounds(S_WAY), rounds(T_WAY)
    at_x = AT_D + n_d
    for tick in range(max(n_rs, AT_D + n_d, AT_S + n_s, AT_T + n_t, AT_X2) + 1):
        if tick <= n_rs:
            rs_step(tick)
        for which in range(2):
            @pl.when(z == which)
            def _(which=which):
                for d in far_first[tick * PER:(tick + 1) * PER]:
                    share(which, d).start()

        if tick == AT_S:
            total, at = Pt[z], -1
            for route in RS_WAY:
                at += len(route) - 1
                total += got[at]
            SG[c, z] = total

            @pl.when(source)
            def _():
                first = jnp.where(y == 0, 1, 0)
                second = jnp.where(y == 2, 1, 2)
                for d in range(1, NX):
                    remote(SG.at[0, z, first], TG.at[0, z, y], t1_s.at[0, d], t1_r, 2 * z, d * NY + y).start()
                for d in range(NX):
                    remote(
                        SG.at[0, z, second], TG.at[1, z, y], t1_s.at[1, d], t1_r, 2 * z + 1, d * NY + y
                    ).start()
                TG[0, z, y] = SG[0, z, first]
        if AT_S <= tick <= AT_S + n_s:
            ag_step("s", S_WAY, smine, tick - AT_S, sg_s, sg_r, to_sibling(smine, fs_s, fs_r))
        if tick == AT_T2:
            @pl.when(y < 3)
            def _():
                piece = TG.at[c, z, y]

                @pl.when(jnp.logical_not(source))
                def _():
                    remote(piece, piece, t1_s.at[0, 0], t1_r, row, y).wait_recv()

                for d in range(1, NY):
                    remote(piece, piece, t2_s.at[d], t2_r.at[y], row, x * NY + (y + d) % NY).start()

        if tick == AT_D:
            @pl.when(z != 0)
            def _():
                remote(B.at[:, 0:ch], DG.at[z, pl.ds(0, 2)], ds_s.at[0], ds_r.at[0], up, q).wait_recv()

            @pl.when(z != 1)
            def _():
                remote(
                    B.at[pl.ds(0, 1), 0:ch], DG.at[z, pl.ds(2, 1)], ds_s.at[0], ds_r.at[1], up, q
                ).wait_recv()
        if AT_D <= tick <= AT_D + n_d:
            ag_step("d", D_WAY, DG, tick - AT_D, dg_s, dg_r)
        if tick == AT_T:
            for j in range(3):
                @pl.when(y != j)
                def _(j=j):
                    piece = TG.at[c, z, j]
                    remote(piece, piece, t2_s.at[0], t2_r.at[j], row, q).wait_recv()
        if AT_T <= tick <= AT_T + n_t:
            ag_step("t", T_WAY, tmine, tick - AT_T, tg_s, tg_r, to_sibling(tmine, ft_s, ft_r))
        if tick == at_x:
            dg = [split3(DG[:, k].reshape(nb, nb)) for k in range(3)]
            for h in range(2):
                moved = jnp.zeros((nb, nb), F32)
                for k in range(3):
                    oh = jnp.broadcast_to(came[h], (nb, nb)) == lanef + float(k * nb)
                    oh = oh.astype(F32).astype(BF16)
                    moved += dot(oh, dg[k][0]) + dot(oh, dg[k][1]) + dot(oh, dg[k][2])
                keep = jnp.broadcast_to(came[h], (nb, nb)) == jnp.broadcast_to(own[h], (nb, nb))
                NBf[h] = jnp.where(keep, B[h], moved)

            @pl.when(source)
            def _():
                for p in range(PX):
                    for h, d, cp in strips(p):
                        cp.start()
                XG[y] = NBf[0]

            crossing.append(begin(remote(NBf.at[1 - c], NX_, nx_s, nx_r, sib, q)))
        if tick == AT_X2:
            @pl.when(y < 3)
            def _():
                for p in range(PX):
                    piece = XG.at[y, part(p)]

                    @pl.when(jnp.logical_not(source))
                    def _(p=p, piece=piece):
                        remote(piece, piece, x1_s.at[0, 0, p], x1_r.at[p], row, y).wait_recv()

                    for d in range(1, NY):
                        strips_y(d, p).start()

    for j in range(3):
        @pl.when(y != j)
        def _(j=j):
            for p in range(PX):
                piece = XG.at[j, part(p)]
                remote(piece, piece, x2_s.at[0, p], x2_r.at[j, p], row, q).wait_recv()
    for cp in crossing:
        cp.wait_recv()

    load_inv.wait()
    i0, i1, i2 = inv_ref[0], inv_ref[1], inv_ref[2]
    t10, t01, t02, t20, t21, t12 = (TG[j // 3, :, j % 3].reshape(nb, nb) for j in range(6))
    l10, l20 = mm(t10, i0), mm(t20, i0)
    l21 = mm(t21 - mm(l20, t01), i1)
    u12 = t12 - mm(l10, t02)
    l0 = mm(XG[0], i0)
    l1 = mm(XG[1] - mm(l0, t01), i1)
    l2 = mm(XG[2] - mm(l0, t02) - mm(l1, u12), i2)
    for h in range(2):
        cols = pl.ds(h * nb, nb)
        s0, s1, s2 = (SG[h, :, k].reshape(nb, nb) for k in range(3))
        u0 = s0
        u1 = s1 - mm(l10, u0)
        u2 = s2 - mm(l20, u0) - mm(l21, u1)

        @pl.when(row >= 3)
        def _(h=h, cols=cols, u0=u0, u1=u1, u2=u2):
            @pl.when(c == h)
            def _():
                o_ref[:, cols] = NBf[h]

            @pl.when(c != h)
            def _():
                o_ref[:, cols] = NX_[...]

            o_ref[:, cols] -= mm(l0, u0) + mm(l1, u1) + mm(l2, u2)

        for r, u in enumerate((u0, u1, u2)):
            @pl.when(row == r)
            def _(cols=cols, u=u):
                o_ref[:, cols] = u
    for k, l in enumerate((l0, l1, l2)):
        @pl.when(jnp.logical_and(row >= 3, q == k))
        def _(l=l):
            o_ref[:, 0:nb] = l
    for r, k, l in ((1, 0, l10), (2, 0, l20), (2, 1, l21)):
        @pl.when(jnp.logical_and(row == r, q == k))
        def _(l=l):
            o_ref[:, 0:nb] = l

    swap.wait_send()
    for cp in sent:
        cp.wait_send()
    for which in range(2):
        @pl.when(z == which)
        def _(which=which):
            for d in range(1, nz):
                share(which, d).wait_send()

    @pl.when(source)
    def _():
        for d in range(1, NX):
            remote(SG.at[0, z, 0], TG.at[0, z, y], t1_s.at[0, d], t1_r, 2 * z, d * NY + y).wait_send()
        for d in range(NX):
            remote(SG.at[0, z, 0], TG.at[1, z, y], t1_s.at[1, d], t1_r, 2 * z + 1, d * NY + y).wait_send()
        for p in range(PX):
            for h, d, cp in strips(p):
                cp.wait_send()

    @pl.when(y < 3)
    def _():
        for d in range(1, NY):
            to = x * NY + (y + d) % NY
            piece = TG.at[c, z, y]
            remote(piece, piece, t2_s.at[d], t2_r.at[y], row, to).wait_send()
            for p in range(PX):
                strips_y(d, p).wait_send()


def on_device(matrix, pivots, inverses):
    nb = inverses.shape[1]
    nz = lax.axis_size("row") // 2
    ch = nb // nz
    DMA = pltpu.SemaphoreType.DMA

    def vm(*shape):
        return pltpu.VMEM(shape, F32)

    return pl.pallas_call(
        functools.partial(kernel, nz, nb),
        out_shape=jax.ShapeDtypeStruct(matrix.shape, matrix.dtype),
        in_specs=[
            pl.BlockSpec(memory_space=pl.ANY),
            pl.BlockSpec(memory_space=pl.ANY),
            pl.BlockSpec(memory_space=pl.ANY),
        ],
        out_specs=pl.BlockSpec(memory_space=pltpu.VMEM),
        scratch_shapes=[
            pltpu.VMEM(pivots.shape, jnp.int32), vm(*inverses.shape), DMA((2,)),
            vm(2, nb, nb), vm(nz, 3, ch, nb), vm(2, nz, 3, ch, nb), vm(nz, 3, ch, nb), vm(2, nz, 3, ch, nb),
            vm(3, nb, nb), vm(2, nb, nb), vm(nb, nb),
            vm(nz - 1, 3, ch, nb), vm(nz - 1, 3, ch, nb),
            DMA, DMA, DMA, DMA((nz,)), DMA((2,)),
            DMA((nz - 1,)), DMA((nz - 1,)), DMA((nz - 1,)), DMA((nz - 1,)),
            DMA((nz - 1,)), DMA((nz - 1,)), DMA((nz - 1,)), DMA((nz - 1,)),
            DMA((nz,)), DMA((nz,)), DMA((nz,)), DMA((nz,)),
            DMA((2, NX)), DMA, DMA((NY,)), DMA((3,)),
            DMA((2, NX, PX)), DMA((PX,)), DMA((NY, PX)), DMA((3, PX)),
            DMA, DMA,
        ],
        compiler_params=pltpu.CompilerParams(
            collective_id=0, has_side_effects=True, vmem_limit_bytes=60 * 2**20
        ),
        name="panels",
    )(matrix, pivots, inverses)


def solution(mesh):
    placed = (P("row", "col"), P(), P())
    return jax.shard_map(
        on_device, mesh=mesh, in_specs=placed, out_specs=P("row", "col"), check_vma=False
    )
```

time: 117 us -> 95.7 us (0.82)
  the two profiles are of different devices: /device:TPU:1 before, /device:TPU:4 now
where the time goes in v2:
time: 95.7 us; the launch traced here: 95.5 us
  Pallas kernels  93.6 us (98%)
  local copies, waits for them, and re-layouts  1.87 us (2%)
    pallas_call x1, Pallas kernels, on_device(): pl.pallas_call(functools.partial(kernel, nz, nb), out_shape=jax.ShapeDtyp...  93.6 us

profile of v2, /device:TPU:4, one launch (start us, length us, event | category | flops | bytes accessed | tf_op | source)
XLA Modules:
  0.0 95.5 jit_solution(5263231211513760256)
XLA Ops:
  0.0 93.6 %panels.1 = f32[256,512]{1,0:T(8,128)} custom-call(f32[256,512]{1,0:T(8,128)} %a_ref.1, s32[3,256]{1,0:T(4,128)} %piv_hbm.1, f32[3,256,256]{2,1,0:T(8,128)} %inv_hbm.1), custom_call_target="tpu_custom_call" | custom-call | tf_op jit(solution)/shard_map/panels/pallas_call | solution.py:421
  93.6 1.9 %copy.5 = f32[256,512]{1,0:T(8,128)} copy(f32[256,512]{1,0:T(8,128)} %panels.1) | data formatting | bytes 1048576

commit v3 on v2

--- a/solution.py
+++ b/solution.py
@@ -13,8 +13,9 @@
 NX, NY = 4, 4
 RING = ((0, 1, 2, 3, 4, 5, 6, 7, 8), (0, -1, -2, -3, -4, -5, -6, -7))
 RS_WAY, D_WAY, S_WAY, T_WAY = RING, RING, RING, RING
-AT_D, AT_S, AT_T2, AT_T, AT_X2 = 4, 8, 9, 10, 15
-PER, PX = 5, 2
+AT_D, AT_S, AT_T2, AT_T, AT_X2 = 4, 8, 9, 10, 14
+RS_CUT, D_CUT, S_CUT, T_CUT = 3, 3, 1, 3
+PER, PX, GAP_X = 5, 2, 2
 
 
 def dot(a, b):
@@ -176,35 +177,47 @@
     def chip(d):
         return 2 * ring(z + d) + c
 
+    def cuts(n):
+        return [(p, pl.ds(p * (3 // n), 3 // n)) for p in range(n)]
+
     def rs_step(t):
-        for w, route in enumerate(RS_WAY):
-            n = len(route) - 1
-            at = sum(len(r) - 1 for r in RS_WAY[:w]) + t
-            if 0 < t <= n:
-                flight.pop(("rs", w)).wait_recv()
-            if t < n:
-                far = route[n - t]
-                i = ring(z + far)
-                put[at] = Pt[i] if t == 0 else Pt[i] + got[at - 1]
-                flight["rs", w] = begin(
-                    remote(put.at[at], got.at[at], rs_s.at[at], rs_r.at[at], chip(far - route[n - t - 1]), q)
-                )
-
-    def ag_step(name, way, buf, t, ss, rs, forward=None):
+        for p, ks in cuts(RS_CUT):
+            for w, route in enumerate(RS_WAY):
+                n = len(route) - 1
+                at = sum(len(r) - 1 for r in RS_WAY[:w]) + t
+                if 0 < t <= n:
+                    flight.pop(("rs", w, p)).wait_recv()
+                if t < n:
+                    far = route[n - t]
+                    i = ring(z + far)
+                    put[at, ks] = Pt[i, ks] if t == 0 else Pt[i, ks] + got[at - 1, ks]
+                    flight["rs", w, p] = begin(
+                        remote(
+                            put.at[at, ks], got.at[at, ks], rs_s.at[at, p], rs_r.at[at, p],
+                            chip(far - route[n - t - 1]), q,
+                        )
+                    )
+
+    def ag_step(name, way, cut, buf, t, ss, rs, forward=None):
         if t == 0 and forward is not None:
             forward(0, z)
+        for p, ks in cuts(cut):
+            for w, route in enumerate(way):
+                n = len(route) - 1
+                at = sum(len(r) - 1 for r in way[:w]) + t
+                if 0 < t <= n:
+                    flight.pop((name, w, p)).wait_recv()
+                if t < n:
+                    i = ring(z - route[t])
+                    flight[name, w, p] = begin(
+                        remote(
+                            buf.at[i, ks], buf.at[i, ks], ss.at[at, p], rs.at[at, p],
+                            chip(route[t + 1] - route[t]), q,
+                        )
+                    )
         for w, route in enumerate(way):
-            n = len(route) - 1
-            at = sum(len(r) - 1 for r in way[:w]) + t
-            if 0 < t <= n:
-                flight.pop((name, w)).wait_recv()
-            if t < n:
-                i = ring(z - route[t])
-                flight[name, w] = begin(
-                    remote(buf.at[i], buf.at[i], ss.at[at], rs.at[at], chip(route[t + 1] - route[t]), q)
-                )
-            if forward is not None and 0 < t <= n:
-                forward(at, z - route[t])
+            if forward is not None and 0 < t <= len(route) - 1:
+                forward(sum(len(r) - 1 for r in way[:w]) + t, z - route[t])
 
     tmine = TG.at[c]
     smine = SG.at[c]
@@ -220,13 +233,12 @@
     def part(p):
         return pl.ds(p * (nb // PX), nb // PX)
 
-    def strips(p):
-        for d in range(NX):
-            for h in range(2):
-                if d or h:
-                    yield h, d, remote(
-                        NBf.at[h, part(p)], XG.at[y, part(p)], x1_s.at[h, d, p], x1_r.at[p], 2 * z + h, d * NY + y
-                    )
+    def strips(h):
+        for p in range(PX):
+            for d in range(1 - h, NX):
+                yield remote(
+                    NBf.at[h, part(p)], XG.at[y, part(p)], x1_s.at[h, d, p], x1_r.at[p], 2 * z + h, d * NY + y
+                )
 
     def strips_y(d, p):
         piece = XG.at[y, part(p)]
@@ -237,7 +249,7 @@
 
     n_rs, n_d, n_s, n_t = rounds(RS_WAY), rounds(D_WAY), rounds(S_WAY), rounds(T_WAY)
     at_x = AT_D + n_d
-    for tick in range(max(n_rs, AT_D + n_d, AT_S + n_s, AT_T + n_t, AT_X2) + 1):
+    for tick in range(max(n_rs, AT_D + n_d, AT_S + n_s, AT_T + n_t, AT_X2 + GAP_X) + 1):
         if tick <= n_rs:
             rs_step(tick)
         for which in range(2):
@@ -265,7 +277,7 @@
                     ).start()
                 TG[0, z, y] = SG[0, z, first]
         if AT_S <= tick <= AT_S + n_s:
-            ag_step("s", S_WAY, smine, tick - AT_S, sg_s, sg_r, to_sibling(smine, fs_s, fs_r))
+            ag_step("s", S_WAY, S_CUT, smine, tick - AT_S, sg_s, sg_r, to_sibling(smine, fs_s, fs_r))
         if tick == AT_T2:
             @pl.when(y < 3)
             def _():
@@ -289,7 +301,7 @@
                     B.at[pl.ds(0, 1), 0:ch], DG.at[z, pl.ds(2, 1)], ds_s.at[0], ds_r.at[1], up, q
                 ).wait_recv()
         if AT_D <= tick <= AT_D + n_d:
-            ag_step("d", D_WAY, DG, tick - AT_D, dg_s, dg_r)
+            ag_step("d", D_WAY, D_CUT, DG, tick - AT_D, dg_s, dg_r)
         if tick == AT_T:
             for j in range(3):
                 @pl.when(y != j)
@@ -297,7 +309,7 @@
                     piece = TG.at[c, z, j]
                     remote(piece, piece, t2_s.at[0], t2_r.at[j], row, q).wait_recv()
         if AT_T <= tick <= AT_T + n_t:
-            ag_step("t", T_WAY, tmine, tick - AT_T, tg_s, tg_r, to_sibling(tmine, ft_s, ft_r))
+            ag_step("t", T_WAY, T_CUT, tmine, tick - AT_T, tg_s, tg_r, to_sibling(tmine, ft_s, ft_r))
         if tick == at_x:
             dg = [split3(DG[:, k].reshape(nb, nb)) for k in range(3)]
             for h in range(2):
@@ -309,26 +321,41 @@
                 keep = jnp.broadcast_to(came[h], (nb, nb)) == jnp.broadcast_to(own[h], (nb, nb))
                 NBf[h] = jnp.where(keep, B[h], moved)
 
-            @pl.when(source)
-            def _():
-                for p in range(PX):
-                    for h, d, cp in strips(p):
+                @pl.when(source)
+                def _(h=h):
+                    for cp in strips(h):
                         cp.start()
-                XG[y] = NBf[0]
+                    if h == 0:
+                        XG[y] = NBf[0]
 
             crossing.append(begin(remote(NBf.at[1 - c], NX_, nx_s, nx_r, sib, q)))
-        if tick == AT_X2:
-            @pl.when(y < 3)
-            def _():
-                for p in range(PX):
+        for p in range(PX):
+            if tick == AT_X2 + p * GAP_X // PX:
+                @pl.when(y < 3)
+                def _(p=p):
                     piece = XG.at[y, part(p)]
 
                     @pl.when(jnp.logical_not(source))
-                    def _(p=p, piece=piece):
+                    def _():
                         remote(piece, piece, x1_s.at[0, 0, p], x1_r.at[p], row, y).wait_recv()
 
                     for d in range(1, NY):
                         strips_y(d, p).start()
+
+    for cp in crossing:
+        cp.wait_recv()
+
+    load_inv.wait()
+    i0, i1, i2 = inv_ref[0], inv_ref[1], inv_ref[2]
+    t10, t01, t02, t20, t21, t12 = (TG[j // 3, :, j % 3].reshape(nb, nb) for j in range(6))
+    l10, l20 = mm(t10, i0), mm(t20, i0)
+    l21 = mm(t21 - mm(l20, t01), i1)
+    u12 = t12 - mm(l10, t02)
+    us = []
+    for h in range(2):
+        s0, s1, s2 = (SG[h, :, k].reshape(nb, nb) for k in range(3))
+        u1 = s1 - mm(l10, s0)
+        us.append((s0, u1, s2 - mm(l20, s0) - mm(l21, u1)))
 
     for j in range(3):
         @pl.when(y != j)
@@ -336,24 +363,12 @@
             for p in range(PX):
                 piece = XG.at[j, part(p)]
                 remote(piece, piece, x2_s.at[0, p], x2_r.at[j, p], row, q).wait_recv()
-    for cp in crossing:
-        cp.wait_recv()
-
-    load_inv.wait()
-    i0, i1, i2 = inv_ref[0], inv_ref[1], inv_ref[2]
-    t10, t01, t02, t20, t21, t12 = (TG[j // 3, :, j % 3].reshape(nb, nb) for j in range(6))
-    l10, l20 = mm(t10, i0), mm(t20, i0)
-    l21 = mm(t21 - mm(l20, t01), i1)
-    u12 = t12 - mm(l10, t02)
     l0 = mm(XG[0], i0)
     l1 = mm(XG[1] - mm(l0, t01), i1)
     l2 = mm(XG[2] - mm(l0, t02) - mm(l1, u12), i2)
     for h in range(2):
         cols = pl.ds(h * nb, nb)
-        s0, s1, s2 = (SG[h, :, k].reshape(nb, nb) for k in range(3))
-        u0 = s0
-        u1 = s1 - mm(l10, u0)
-        u2 = s2 - mm(l20, u0) - mm(l21, u1)
+        u0, u1, u2 = us[h]
 
         @pl.when(row >= 3)
         def _(h=h, cols=cols, u0=u0, u1=u1, u2=u2):
@@ -395,8 +410,8 @@
             remote(SG.at[0, z, 0], TG.at[0, z, y], t1_s.at[0, d], t1_r, 2 * z, d * NY + y).wait_send()
         for d in range(NX):
             remote(SG.at[0, z, 0], TG.at[1, z, y], t1_s.at[1, d], t1_r, 2 * z + 1, d * NY + y).wait_send()
-        for p in range(PX):
-            for h, d, cp in strips(p):
+        for h in range(2):
+            for cp in strips(h):
                 cp.wait_send()
 
     @pl.when(y < 3)
@@ -433,8 +448,8 @@
             vm(3, nb, nb), vm(2, nb, nb), vm(nb, nb),
             vm(nz - 1, 3, ch, nb), vm(nz - 1, 3, ch, nb),
             DMA, DMA, DMA, DMA((nz,)), DMA((2,)),
-            DMA((nz - 1,)), DMA((nz - 1,)), DMA((nz - 1,)), DMA((nz - 1,)),
-            DMA((nz - 1,)), DMA((nz - 1,)), DMA((nz - 1,)), DMA((nz - 1,)),
+            DMA((nz - 1, 3)), DMA((nz - 1, 3)), DMA((nz - 1, 3)), DMA((nz - 1, 3)),
+            DMA((nz - 1, 3)), DMA((nz - 1, 3)), DMA((nz - 1, 3)), DMA((nz - 1, 3)),
             DMA((nz,)), DMA((nz,)), DMA((nz,)), DMA((nz,)),
             DMA((2, NX)), DMA, DMA((NY,)), DMA((3,)),
             DMA((2, NX, PX)), DMA((PX,)), DMA((NY, PX)), DMA((3, PX)),

time: 95.7 us -> 92.8 us (0.970)
  the two profiles are of different devices: /device:TPU:4 before, /device:TPU:1 now
where the time goes in v3:
time: 92.8 us; the launch traced here: 92.6 us
  Pallas kernels  90.7 us (98%)
  local copies, waits for them, and re-layouts  1.87 us (2%)
    pallas_call x1, Pallas kernels, on_device(): pl.pallas_call(functools.partial(kernel, nz, nb), out_shape=jax.ShapeDtyp...  90.7 us
    unnamed x1, local copies, waits for them, and re-layouts  1.87 us

profile of v3, /device:TPU:1, one launch (start us, length us, event | category | flops | bytes accessed | tf_op | source)
XLA Modules:
  0.0 92.6 jit_solution(16099043426839101183)
XLA Ops:
  0.0 90.7 %panels.1 = f32[256,512]{1,0:T(8,128)} custom-call(f32[256,512]{1,0:T(8,128)} %a_ref.1, s32[3,256]{1,0:T(4,128)} %piv_hbm.1, f32[3,256,256]{2,1,0:T(8,128)} %inv_hbm.1), custom_call_target="tpu_custom_call" | custom-call | tf_op jit(solution)/shard_map/panels/pallas_call | solution.py:436
  90.7 1.9 %copy.5 = f32[256,512]{1,0:T(8,128)} copy(f32[256,512]{1,0:T(8,128)} %panels.1) | data formatting | bytes 1048576

commit v4 on v3

--- a/solution.py
+++ b/solution.py
@@ -276,8 +276,6 @@
                         SG.at[0, z, second], TG.at[1, z, y], t1_s.at[1, d], t1_r, 2 * z + 1, d * NY + y
                     ).start()
                 TG[0, z, y] = SG[0, z, first]
-        if AT_S <= tick <= AT_S + n_s:
-            ag_step("s", S_WAY, S_CUT, smine, tick - AT_S, sg_s, sg_r, to_sibling(smine, fs_s, fs_r))
         if tick == AT_T2:
             @pl.when(y < 3)
             def _():
@@ -290,18 +288,6 @@
                 for d in range(1, NY):
                     remote(piece, piece, t2_s.at[d], t2_r.at[y], row, x * NY + (y + d) % NY).start()
 
-        if tick == AT_D:
-            @pl.when(z != 0)
-            def _():
-                remote(B.at[:, 0:ch], DG.at[z, pl.ds(0, 2)], ds_s.at[0], ds_r.at[0], up, q).wait_recv()
-
-            @pl.when(z != 1)
-            def _():
-                remote(
-                    B.at[pl.ds(0, 1), 0:ch], DG.at[z, pl.ds(2, 1)], ds_s.at[0], ds_r.at[1], up, q
-                ).wait_recv()
-        if AT_D <= tick <= AT_D + n_d:
-            ag_step("d", D_WAY, D_CUT, DG, tick - AT_D, dg_s, dg_r)
         if tick == AT_T:
             for j in range(3):
                 @pl.when(y != j)
@@ -310,6 +296,20 @@
                     remote(piece, piece, t2_s.at[0], t2_r.at[j], row, q).wait_recv()
         if AT_T <= tick <= AT_T + n_t:
             ag_step("t", T_WAY, T_CUT, tmine, tick - AT_T, tg_s, tg_r, to_sibling(tmine, ft_s, ft_r))
+        if AT_S <= tick <= AT_S + n_s:
+            ag_step("s", S_WAY, S_CUT, smine, tick - AT_S, sg_s, sg_r, to_sibling(smine, fs_s, fs_r))
+        if tick == AT_D:
+            @pl.when(z != 0)
+            def _():
+                remote(B.at[:, 0:ch], DG.at[z, pl.ds(0, 2)], ds_s.at[0], ds_r.at[0], up, q).wait_recv()
+
+            @pl.when(z != 1)
+            def _():
+                remote(
+                    B.at[pl.ds(0, 1), 0:ch], DG.at[z, pl.ds(2, 1)], ds_s.at[0], ds_r.at[1], up, q
+                ).wait_recv()
+        if AT_D <= tick <= AT_D + n_d:
+            ag_step("d", D_WAY, D_CUT, DG, tick - AT_D, dg_s, dg_r)
         if tick == at_x:
             dg = [split3(DG[:, k].reshape(nb, nb)) for k in range(3)]
             for h in range(2):

time: 92.8 us -> 91.7 us (0.988)
  Pallas kernels: 90.7 us -> 89.6 us
    pallas_call x1, Pallas kernels: 90.7 us -> 89.6 us  [on_device(): pl.pallas_call(functools.partial(kernel, nz, nb), out_shape=jax.ShapeDtyp...]
where the time goes in v4:
time: 91.7 us; the launch traced here: 91.5 us
  Pallas kernels  89.6 us (98%)
  local copies, waits for them, and re-layouts  1.87 us (2%)
    pallas_call x1, Pallas kernels, on_device(): pl.pallas_call(functools.partial(kernel, nz, nb), out_shape=jax.ShapeDtyp...  89.6 us
    unnamed x1, local copies, waits for them, and re-layouts  1.87 us

profile of v4, /device:TPU:1, one launch (start us, length us, event | category | flops | bytes accessed | tf_op | source)
XLA Modules:
  0.0 91.5 jit_solution(6152792175372043097)
XLA Ops:
  0.0 89.6 %panels.1 = f32[256,512]{1,0:T(8,128)} custom-call(f32[256,512]{1,0:T(8,128)} %a_ref.1, s32[3,256]{1,0:T(4,128)} %piv_hbm.1, f32[3,256,256]{2,1,0:T(8,128)} %inv_hbm.1), custom_call_target="tpu_custom_call" | custom-call | tf_op jit(solution)/shard_map/panels/pallas_call | solution.py:436
  89.7 1.9 %copy.5 = f32[256,512]{1,0:T(8,128)} copy(f32[256,512]{1,0:T(8,128)} %panels.1) | data formatting | bytes 1048576

commit v5 on v4

--- a/solution.py
+++ b/solution.py
@@ -296,8 +296,6 @@
                     remote(piece, piece, t2_s.at[0], t2_r.at[j], row, q).wait_recv()
         if AT_T <= tick <= AT_T + n_t:
             ag_step("t", T_WAY, T_CUT, tmine, tick - AT_T, tg_s, tg_r, to_sibling(tmine, ft_s, ft_r))
-        if AT_S <= tick <= AT_S + n_s:
-            ag_step("s", S_WAY, S_CUT, smine, tick - AT_S, sg_s, sg_r, to_sibling(smine, fs_s, fs_r))
         if tick == AT_D:
             @pl.when(z != 0)
             def _():
@@ -310,6 +308,8 @@
                 ).wait_recv()
         if AT_D <= tick <= AT_D + n_d:
             ag_step("d", D_WAY, D_CUT, DG, tick - AT_D, dg_s, dg_r)
+        if AT_S <= tick <= AT_S + n_s:
+            ag_step("s", S_WAY, S_CUT, smine, tick - AT_S, sg_s, sg_r, to_sibling(smine, fs_s, fs_r))
         if tick == at_x:
             dg = [split3(DG[:, k].reshape(nb, nb)) for k in range(3)]
             for h in range(2):

time: 91.7 us -> 93 us (1.014)
  Pallas kernels: 89.6 us -> 90.9 us
    pallas_call x1, Pallas kernels: 89.6 us -> 90.9 us  [on_device(): pl.pallas_call(functools.partial(kernel, nz, nb), out_shape=jax.ShapeDtyp...]
where the time goes in v5:
time: 93 us; the launch traced here: 92.8 us
  Pallas kernels  90.9 us (98%)
  local copies, waits for them, and re-layouts  1.87 us (2%)
    pallas_call x1, Pallas kernels, on_device(): pl.pallas_call(functools.partial(kernel, nz, nb), out_shape=jax.ShapeDtyp...  90.9 us
    unnamed x1, local copies, waits for them, and re-layouts  1.87 us

profile of v5, /device:TPU:1, one launch (start us, length us, event | category | flops | bytes accessed | tf_op | source)
XLA Modules:
  0.0 92.8 jit_solution(15582792964556203517)
XLA Ops:
  0.0 90.9 %panels.1 = f32[256,512]{1,0:T(8,128)} custom-call(f32[256,512]{1,0:T(8,128)} %a_ref.1, s32[3,256]{1,0:T(4,128)} %piv_hbm.1, f32[3,256,256]{2,1,0:T(8,128)} %inv_hbm.1), custom_call_target="tpu_custom_call" | custom-call | tf_op jit(solution)/shard_map/panels/pallas_call | solution.py:436
  90.9 1.9 %copy.5 = f32[256,512]{1,0:T(8,128)} copy(f32[256,512]{1,0:T(8,128)} %panels.1) | data formatting | bytes 1048576
